TPU v7x, 128 devices: a whole 4x4x4 slice. The times are simulated.
128 devices in a mesh: prefix: 16 (over z, x), row: 8 (over y, core).
Axes of the slice: x: 4, y: 4, z: 4, core: 2. Of those that a mesh axis runs over, the one named last changes fastest.
Arguments:
- queries: bfloat16 [1024, 8192], P(('prefix', 'row')), may hold values from -32 to 32
- prefix_ids: int32 [1024], P(('prefix', 'row')), may hold values from 0 to 15, as said below
- prefix_lengths: int32 [16], P('prefix'), may hold values from 1 to 16384, 65536 in all
- prefix_keys: bfloat16 [16, 8, 16384, 128], P('prefix', None, 'row'), may hold values from -12 to 12
- prefix_values: bfloat16 [16, 8, 16384, 128], P('prefix', None, 'row'), may hold values from -6 to 6
- suffix_keys: bfloat16 [1024, 8, 512, 128], P(('prefix', 'row')), may hold values from -12 to 12
- suffix_values: bfloat16 [1024, 8, 512, 128], P(('prefix', 'row')), may hold values from -6 to 6
- suffix_lengths: int32 [1024], P(('prefix', 'row')), may hold values from 1 to 512, 393216 in all
Outputs:
- attended: bfloat16 [1024, 8192], P(('prefix', 'row'))
Inputs may be any that keep to these rules, and one draw needn't show every extreme that they name: `prefix_ids`: each block of 8 requests held by one device names any prefix at most 2 times, and one prefix is named exactly 2 times in every block.
All inputs are finite; a program needn't handle non-finite values. No bound on the sum of `prefix_lengths` or of `suffix_lengths` on one device may be relied on, other than what follows from the above.
Results may differ from a plain program's by a relative error of at most 0.01.
Values may be sent and summed in bfloat16 or wider, within the bound.
No kernel may reach another device: no remote copies, remote signals or barrier semaphores. Data moves between devices by JAX's collectives and lax.ppermute only.
A program may use at most 320 MiB of HBM per device.

v0:
```python
import math

import jax
import jax.numpy as jnp
from jax import lax
from jax.sharding import PartitionSpec as P

CAP = 2


MASKED = -1e30


def block_partials(slot_rows, keys_here, values_here, length, first_token):
    slot_count = slot_rows.shape[0]
    kv_heads = keys_here.shape[1]
    token_span = keys_here.shape[2]
    head_dim = keys_here.shape[3]
    groups = slot_rows.shape[1] // (kv_heads * head_dim)
    scaling = 1.0 / math.sqrt(head_dim)
    position = first_token + jnp.arange(token_span, dtype=jnp.int32)
    is_valid = (position < length)[None, :]
    grouped = slot_rows.reshape(slot_count, kv_heads, groups * head_dim)
    maxima, totals, outputs = ([], [], [])
    for kv_index in range(kv_heads):
        query_rows = grouped[:, kv_index].reshape(slot_count * groups, head_dim)
        scores = (
            lax.dot_general(
                query_rows,
                keys_here[0, kv_index],
                (((1,), (1,)), ((), ())),
                preferred_element_type=jnp.float32,
            )
            * scaling
        )
        block_max = jnp.max(jnp.where(is_valid, scores, MASKED), axis=1)
        weights = jnp.where(is_valid, jnp.exp(scores - block_max[:, None]), 0.0)
        totals.append(jnp.sum(weights, axis=1).reshape(slot_count, groups))
        maxima.append(block_max.reshape(slot_count, groups))
        product = jnp.dot(
            weights.astype(jnp.bfloat16),
            values_here[0, kv_index],
            preferred_element_type=jnp.float32,
        )
        outputs.append(product.reshape(slot_count, groups, head_dim))
    head_count = kv_heads * groups
    return (
        jnp.stack(maxima, 1).reshape(slot_count, head_count),
        jnp.stack(totals, 1).reshape(slot_count, head_count),
        jnp.stack(outputs, 1).reshape(slot_count, head_count, head_dim),
    )


def suffix_partials(queries, suffix_keys, suffix_values, suffix_lengths):
    row_count = queries.shape[0]
    kv_heads = suffix_keys.shape[1]
    token_span = suffix_keys.shape[2]
    head_dim = suffix_keys.shape[3]
    groups = queries.shape[1] // (kv_heads * head_dim)
    scaling = 1.0 / math.sqrt(head_dim)
    grouped = queries.reshape(row_count, kv_heads, groups, head_dim)
    scores = (
        jnp.einsum("rkgd,rktd->rkgt", grouped, suffix_keys, preferred_element_type=jnp.float32)
        * scaling
    )
    is_valid = (jnp.arange(token_span, dtype=jnp.int32)[None, :] < suffix_lengths[:, None])[
        :, None, None, :
    ]
    suffix_peak = jnp.max(jnp.where(is_valid, scores, MASKED), axis=3)
    weights = jnp.where(is_valid, jnp.exp(scores - suffix_peak[..., None]), 0.0)
    suffix_total = jnp.sum(weights, axis=3)
    suffix_output = jnp.einsum(
        "rkgt,rktd->rkgd",
        weights.astype(jnp.bfloat16),
        suffix_values,
        preferred_element_type=jnp.float32,
    )
    head_count = kv_heads * groups
    return (
        suffix_peak.reshape(row_count, head_count),
        suffix_total.reshape(row_count, head_count),
        suffix_output.reshape(row_count, head_count, head_dim),
    )


def local(
    queries,
    prefix_ids,
    prefix_lengths,
    prefix_keys,
    prefix_values,
    suffix_keys,
    suffix_values,
    suffix_lengths,
):
    owners = lax.axis_size("prefix")
    members = lax.axis_size("row")
    row_count = queries.shape[0]
    row_width = queries.shape[1]
    head_dim = prefix_keys.shape[3]
    head_count = row_width // head_dim
    places = owners * CAP
    ordinal = jnp.arange(row_count, dtype=jnp.int32)
    earlier = (prefix_ids[:, None] == prefix_ids[None, :]) & (ordinal[None, :] < ordinal[:, None])
    target = prefix_ids * CAP + jnp.sum(earlier.astype(jnp.int32), axis=1)
    placing = (jnp.arange(places, dtype=jnp.int32)[:, None] == target[None, :]).astype(jnp.bfloat16)
    outgoing = (
        jnp.dot(placing, queries, preferred_element_type=jnp.float32)
        .astype(jnp.bfloat16)
        .reshape(owners, CAP, row_width)
    )
    suffix_peak, suffix_total, suffix_output = suffix_partials(
        queries, suffix_keys, suffix_values, suffix_lengths
    )
    length = prefix_lengths[0]
    first_token = lax.axis_index("row") * prefix_keys.shape[2]
    copies = jnp.broadcast_to(outgoing[:, None], (owners, members, CAP, row_width)).reshape(
        owners * members, CAP, row_width
    )
    arrived = lax.all_to_all(copies, ("prefix", "row"), split_axis=0, concat_axis=0, tiled=True)
    block_max, block_sum, block_out = block_partials(
        arrived.reshape(-1, row_width), prefix_keys, prefix_values, length, first_token
    )
    back_out, back_sum, back_max = (
        lax.all_to_all(
            block_out.reshape(owners * members, CAP, head_count * head_dim),
            ("prefix", "row"),
            split_axis=0,
            concat_axis=0,
            tiled=True,
        ),
        lax.all_to_all(
            block_sum.reshape(owners * members, CAP, head_count),
            ("prefix", "row"),
            split_axis=0,
            concat_axis=0,
            tiled=True,
        ),
        lax.all_to_all(
            block_max.reshape(owners * members, CAP, head_count),
            ("prefix", "row"),
            split_axis=0,
            concat_axis=0,
            tiled=True,
        ),
    )
    back_max = back_max.reshape(owners, members, CAP, head_count)
    group_max = jnp.max(back_max, axis=1)
    factor = jnp.exp(back_max - group_max[:, None])
    prefix_sum = jnp.sum(
        back_sum.reshape(owners, members, CAP, head_count) * factor, axis=1
    ).reshape(places, head_count)
    prefix_out = jnp.sum(
        back_out.reshape(owners, members, CAP, head_count, head_dim) * factor[..., None], axis=1
    ).reshape(places, head_count, head_dim)
    prefix_max = group_max.reshape(places, head_count)
    pick_max = jnp.take(prefix_max, target, axis=0)
    pick_sum = jnp.take(prefix_sum, target, axis=0)
    pick_out = jnp.take(prefix_out, target, axis=0)
    highest = jnp.maximum(pick_max, suffix_peak)
    prefix_scale = jnp.exp(pick_max - highest)
    suffix_scale = jnp.exp(suffix_peak - highest)
    numerator = prefix_scale[..., None] * pick_out + suffix_scale[..., None] * suffix_output
    denominator = prefix_scale * pick_sum + suffix_scale * suffix_total
    return (numerator / denominator[..., None]).reshape(row_count, row_width).astype(jnp.bfloat16)


def solution(mesh):
    placed = (
        P(("prefix", "row"), None),
        P(("prefix", "row")),
        P("prefix"),
        P("prefix", None, "row", None),
        P("prefix", None, "row", None),
        P(("prefix", "row"), None, None, None),
        P(("prefix", "row"), None, None, None),
        P(("prefix", "row")),
    )
    return jax.shard_map(
        local, mesh=mesh, in_specs=placed, out_specs=P(("prefix", "row"), None), check_vma=False
    )
```

profile of v0, /device:TPU:1, one launch (start us, length us, event | category | flops | bytes accessed | tf_op | source)
XLA Modules:
  0.0 514.2 jit_solution(10652679051215397221)
XLA Ops:
  0.0 0.9 convert_reduce_fusion
  0.9 1.2 compare_and_fusion
  2.1 0.6 copy-done.7
  2.7 1.2 convolution_convert_fusion
  3.9 0.3 broadcast_in_dim.145
  4.2 6.1 %broadcast_in_dim.146 = bf16[16,8,2,8192]{3,2,1,0:T(2,128)(2,1)} broadcast(bf16[16,2,8192]{2,1,0:T(2,128)(2,1)S(1)} %broadcast_in_dim.145), dimensions={0,2,3} | broadcast | bytes 4718592 | tf_op jit(solution)/shard_map/broadcast_in_dim | solution.py:117
  10.3 12.6 %all-to-all-start = ((bf16[128,2,8192]{2,1,0:T(2,128)(2,1)}), bf16[128,2,8192]{2,1,0:T(2,128)(2,1)}, u32[]{:S(2)}, u32[]{:S(2)}) async-start(bf16[128,2,8192]{2,1,0:T(2,128)(2,1)} %bitcast.215), calls=%async_computation | async-start | bytes 8388608 | tf_op jit(solution)/shard_map/all_to_all | solution.py:120
  23.6 52.0 %all-to-all-done = bf16[128,2,8192]{2,1,0:T(2,128)(2,1)} async-done(((bf16[128,2,8192]{2,1,0:T(2,128)(2,1)}), bf16[128,2,8192]{2,1,0:T(2,128)(2,1)}, u32[]{:S(2)}, u32[]{:S(2)}) %all-to-all-start) | async-done | bytes 4194336 | tf_op jit(solution)/shard_map/all_to_all | solution.py:120
  75.6 7.8 %reshape_reshape.12 = bf16[256,8,1024]{2,1,0:T(8,128)(2,1)} reshape(bf16[128,2,8192]{2,1,0:T(2,128)(2,1)} %all-to-all-done) | data formatting | bytes 8388608 | tf_op jit(solution)/shard_map/reshape;reshape | solution.py:23
  83.3 48.9 %slice_reduce_fusion = (bf16[256,1024]{1,0:T(8,128)(2,1)S(1)}, bf16[256,1024]{1,0:T(8,128)(2,1)S(1)}, bf16[256,1024]{1,0:T(8,128)(2,1)S(1)}, bf16[256,1024]{1,0:...) fusion(bf16[256,8,1024]{2,1,0:T(8,128)(2,1)} %reshape_reshape.12), kind=kLoop, calls=%fused_computation.79 | loop fusion | bytes 8388608 | tf_op jit(solution)/shard_map/slice | solution.py:26
  132.2 0.2 reshape_squeeze.24
  132.4 0.2 reshape_squeeze.31
  132.7 3.4 fusion.121
  136.1 10.4 %select_reduce_fusion = (f32[2048]{0:T(1024)S(1)}, f32[2048]{0:T(1024)S(1)}, f32[2048,2048]{1,0:T(8,128)}) fusion(pred[2048]{0:T(1024)(128)(4,1)S(1)} %add_compare_fusion, f32[2048,2048]{1,0:T(8,128)S(1)} %fusion.121, bf16[2048,128]{1,0:T(8,128)(2,1)S(1)} %reshape_squeeze.31, bf16[1,8,2048,128]{3,2,1,0:T(8,128)(2,1)} %param.13), kind=kOutput, calls=%fused_computation.11 | convolution fusion | flops 1098903552 | bytes 34621440 | tf_op jit(solution)/shard_map/dot_general | solution.py:28
  146.5 0.4 copy-done
  146.8 0.8 stack_reshape.56
  147.6 9.8 %fusion.93 = f32[256,8,8,128]{3,2,0,1:T(8,128)} fusion(f32[2048,2048]{1,0:T(8,128)} %copy-done, f32[2048]{0:T(1024)S(1)} %get-tuple-element.29, pred[2048]{0:T(1024)(128)(4,1)S(1)} %add_compare_fusion, bf16[1,8,2048,128]{3,2,1,0:T(8,128)(2,1)} %param.14), kind=kOutput, calls=%fused_computation.77 | convolution fusion | flops 1090519040 | bytes 18360320 | tf_op jit(solution)/shard_map/dot_general | solution.py:40
  157.4 0.2 reshape_squeeze.26
  157.7 9.2 %fusion.117 = f32[2048,2048]{1,0:T(8,128)} fusion(bf16[2048,128]{1,0:T(8,128)(2,1)S(1)} %reshape_squeeze.26, bf16[1,8,2048,128]{3,2,1,0:T(8,128)(2,1)} %param.13), kind=kOutput, calls=%fused_computation.109 | convolution fusion | flops 1073741824 | bytes 17825792 | tf_op jit(solution)/shard_map/dot_general | solution.py:28
  166.9 0.2 reshape_squeeze.27
  167.1 9.2 %fusion.115 = f32[2048,2048]{1,0:T(8,128)} fusion(bf16[2048,128]{1,0:T(8,128)(2,1)S(1)} %reshape_squeeze.27, bf16[1,8,2048,128]{3,2,1,0:T(8,128)(2,1)} %param.13), kind=kOutput, calls=%fused_computation.107 | convolution fusion | flops 1073741824 | bytes 17825792 | tf_op jit(solution)/shard_map/dot_general | solution.py:28
  176.3 0.2 reshape_squeeze.28
  176.5 9.1 %fusion.113 = f32[2048,2048]{1,0:T(8,128)} fusion(bf16[2048,128]{1,0:T(8,128)(2,1)S(1)} %reshape_squeeze.28, bf16[1,8,2048,128]{3,2,1,0:T(8,128)(2,1)} %param.13), kind=kOutput, calls=%fused_computation.105 | convolution fusion | flops 1073741824 | bytes 17825792 | tf_op jit(solution)/shard_map/dot_general | solution.py:28
  185.6 0.2 reshape_squeeze.29
  185.9 9.5 %fusion.111 = f32[2048,2048]{1,0:T(8,128)} fusion(bf16[2048,128]{1,0:T(8,128)(2,1)S(1)} %reshape_squeeze.29, bf16[1,8,2048,128]{3,2,1,0:T(8,128)(2,1)} %param.13), kind=kOutput, calls=%fused_computation.103 | convolution fusion | flops 1073741824 | bytes 17825792 | tf_op jit(solution)/shard_map/dot_general | solution.py:28
  195.4 0.2 reshape_squeeze.30
  195.6 9.1 %fusion.109 = f32[2048,2048]{1,0:T(8,128)} fusion(bf16[2048,128]{1,0:T(8,128)(2,1)S(1)} %reshape_squeeze.30, bf16[1,8,2048,128]{3,2,1,0:T(8,128)(2,1)} %param.13), kind=kOutput, calls=%fused_computation.101 | convolution fusion | flops 1073741824 | bytes 17825792 | tf_op jit(solution)/shard_map/dot_general | solution.py:28
  204.7 0.2 reshape_squeeze.25
  205.0 44.9 %fusion.14 = (f32[2048]{0:T(1024)S(1)}, f32[2048]{0:T(1024)S(1)}, f32[2048]{0:T(1024)S(1)}, f32[2048]{0:T(1024)S(1)}, f32[2048]{0:T(1024)S(1)}, /*index=5*/f32[2...) fusion(f32[2048,2048]{1,0:T(8,128)} %get-tuple-element.39, f32[2048]{0:T(1024)S(1)} %get-tuple-element.28, ...), kind=kOutput, calls=%fused_computation.33 | convolution fusion | flops 1182777344 | bytes 135350272 | tf_op jit(solution)/shard_map/dot_general | solution.py:28
  250.5 35.6 %fusion.12 = (f32[2048]{0:T(1024)S(1)}, f32[2048]{0:T(1024)S(1)}, f32[2048]{0:T(1024)S(1)}, f32[2048]{0:T(1024)S(1)}, f32[2048]{0:T(1024)S(1)}, /*index=5*/f32[2048]{0:T(1024)S(1)}) fusion(f32[2048,2048]{1,0:T(8,128)} %fusion.109, f32[2048]{0:T(1024)S(1)} %get-tuple-element.20, pred[2048]{0:T(1024)(128)(4,1)S(1)} %add_compare_fusion, ...), kind=kLoop, calls=%fused_computation.31 | loop fusion | flops 100651008 | bytes 100763648 | tf_op jit(solution)/shard_map/reduce_sum | solution.py:38
  286.2 10.0 %fusion.87 = f32[256,8,8,128]{3,2,0,1:T(8,128)} fusion(f32[256,8,8,128]{3,2,0,1:T(8,128)} %fusion.93, f32[2048,2048]{1,0:T(8,128)} %get-tuple-element.40, f32[2048]{0:T(1024)S(1)} %get-tuple-element.15, pred[2048]{0:T(1024)(128)(4,1)S(1)} %add_compare_fusion, bf16[1,8,2048,128]{3,2,1,0:T(8,128)(2,1)} %param.14), kind=kOutput, calls=%fused_computation.75 | convolution fusion | flops 1090519040 | bytes 18360320 | tf_op jit(solution)/shard_map/dot_general | solution.py:40
  296.1 9.9 %fusion.81 = f32[256,8,8,128]{3,2,0,1:T(8,128)} fusion(f32[256,8,8,128]{3,2,0,1:T(8,128)} %fusion.87, f32[2048,2048]{1,0:T(8,128)} %fusion.117, f32[2048]{0:T(1024)S(1)} %get-tuple-element.16, pred[2048]{0:T(1024)(128)(4,1)S(1)} %add_compare_fusion, bf16[1,8,2048,128]{3,2,1,0:T(8,128)(2,1)} %param.14), kind=kOutput, calls=%fused_computation.73 | convolution fusion | flops 1090519040 | bytes 18360320 | tf_op jit(solution)/shard_map/dot_general | solution.py:40
  306.1 5.0 fusion.75
  311.1 9.9 %fusion.69 = f32[256,8,8,128]{3,2,0,1:T(8,128)} fusion(f32[256,8,8,128]{3,2,0,1:T(8,128)} %fusion.75, f32[2048,2048]{1,0:T(8,128)} %fusion.113, f32[2048]{0:T(1024)S(1)} %get-tuple-element.18, pred[2048]{0:T(1024)(128)(4,1)S(1)} %add_compare_fusion, bf16[1,8,2048,128]{3,2,1,0:T(8,128)(2,1)} %param.14), kind=kOutput, calls=%fused_computation.69 | convolution fusion | flops 1090519040 | bytes 18360320 | tf_op jit(solution)/shard_map/dot_general | solution.py:40
  321.0 9.9 %fusion.63 = f32[256,8,8,128]{3,2,0,1:T(8,128)} fusion(f32[256,8,8,128]{3,2,0,1:T(8,128)} %fusion.69, f32[2048,2048]{1,0:T(8,128)} %fusion.111, f32[2048]{0:T(1024)S(1)} %get-tuple-element.19, pred[2048]{0:T(1024)(128)(4,1)S(1)} %add_compare_fusion, bf16[1,8,2048,128]{3,2,1,0:T(8,128)(2,1)} %param.14), kind=kOutput, calls=%fused_computation.67 | convolution fusion | flops 1090519040 | bytes 18360320 | tf_op jit(solution)/shard_map/dot_general | solution.py:40
  331.0 4.8 fusion.57
  336.8 0.6 copy.71
  337.4 0.4 reshape_reshape.15
  337.9 0.8 reshape.210
  338.7 4.5 all-to-all-start.3
  343.3 0.6 copy.66
  344.0 0.4 reshape_reshape.13
  344.4 0.8 reshape.208
  345.2 7.7 %all-to-all-done.3 = f32[128,1,128]{2,1,0:T(1,128)S(1)} async-done(((f32[128,1,128]{2,1,0:T(1,128)}), f32[128,1,128]{2,1,0:T(1,128)S(1)}, u32[]{:S(2)}, u32[]{:S(2)}) %all-to-all-start.3) | async-done | bytes 65568 | tf_op jit(solution)/shard_map/all_to_all | solution.py:132
  352.9 4.4 all-to-all-start.1
  357.3 9.8 %fusion.51 = f32[256,8,8,128]{3,2,0,1:T(8,128)} fusion(f32[256,8,8,128]{3,2,0,1:T(8,128)} %fusion.57, f32[2048,2048]{1,0:T(8,128)} %get-tuple-element.39, f32[2048]{0:T(1024)S(1)} %get-tuple-element.28, pred[2048]{0:T(1024)(128)(4,1)S(1)} %add_compare_fusion, bf16[1,8,2048,128]{3,2,1,0:T(8,128)(2,1)} %param.14), kind=kOutput, calls=%fused_computation.63 | convolution fusion | flops 1090519040 | bytes 18360320 | tf_op jit(solution)/shard_map/dot_general | solution.py:40
  367.1 7.8 %copy.69 = f32[256,8,8,128]{3,2,1,0:T(8,128)} copy(f32[256,8,8,128]{3,2,0,1:T(8,128)} %fusion.51) | data formatting | bytes 16777216 | tf_op jit(solution)/shard_map/stack | solution.py:50
  374.9 10.6 %reshape_reshape.14 = f32[128,2,8192]{2,1,0:T(2,128)} reshape(f32[256,8,8,128]{3,2,1,0:T(8,128)} %copy.69) | data formatting | bytes 16777216 | tf_op jit(solution)/shard_map/reshape;reshape | solution.py:126
  385.5 10.7 %all-to-all-start.2 = ((f32[128,2,8192]{2,1,0:T(2,128)}), f32[128,2,8192]{2,1,0:T(2,128)}, u32[]{:S(2)}, u32[]{:S(2)}) async-start(f32[128,2,8192]{2,1,0:T(2,128)} %reshape_reshape.14), calls=%async_computation.2 | async-start | bytes 16777216 | tf_op jit(solution)/shard_map/all_to_all | solution.py:125
  396.3 5.7 %select_reduce_fusion.8 = (f32[8,8,8]{2,1,0:T(8,128)S(1)}, f32[8,8,8,512]{3,2,1,0:T(8,128)S(1)}) fusion(pred[8,512]{1,0:T(8,128)(4,1)S(1)} %iota_compare_fusion, bf16[8,8,512,128]{3,2,1,0:T(8,128)(2,1)} %param.15, bf16[8,8,8,128]{3,0,2,1:T(8,128)(2,1)S(1)} %bitcast.218), kind=kOutput, calls=%fused_computation.88 | convolution fusion | flops 67894784 | bytes 9574400 | tf_op jit(solution)/shard_map/rkgd,rktd->rkgt/dot_general | solution.py:63
  402.1 0.4 fusion.96
  402.6 4.6 convolution_bitcast_fusion
  407.2 0.5 broadcast.174
  407.7 0.8 reduce.16
  408.5 0.1 reshape.211
  408.7 0.8 reduce.17
  409.7 0.1 multiply_reduce_fusion.1
  409.8 0.6 gather_fusion.2
  410.4 0.6 gather_fusion.1
  411.3 83.7 %all-to-all-done.2 = f32[128,2,8192]{2,1,0:T(2,128)} async-done(((f32[128,2,8192]{2,1,0:T(2,128)}), f32[128,2,8192]{2,1,0:T(2,128)}, u32[]{:S(2)}, u32[]{:S(2)}) %all-to-all-start.2) | async-done | bytes 8388640 | tf_op jit(solution)/shard_map/all_to_all | solution.py:125
  495.0 11.8 %reshape.155 = f32[16,8,2,64,128]{4,3,2,1,0:T(8,128)} reshape(f32[128,2,8192]{2,1,0:T(2,128)} %all-to-all-done.2) | data formatting | bytes 16777216 | tf_op jit(solution)/shard_map/reshape | solution.py:154
  506.8 5.3 %multiply_reduce_fusion = f32[16,2,64,128]{3,2,1,0:T(8,128)S(1)} fusion(f32[16,8,2,64,128]{4,3,2,1,0:T(8,128)} %reshape.155, f32[16,8,2,64]{3,2,1,0:T(2,128)S(1)} %get-tuple-element.34), kind=kLoop, calls=%fused_computation.44 | loop fusion | flops 3932160 | bytes 9502720 | tf_op jit(solution)/shard_map/reduce_sum | solution.py:153
  512.1 0.6 gather_fusion
  512.6 1.0 fusion.144
  (80 shorter events, 2.5 us)
Async XLA Ops:
  2.1 0.6 copy-start.7
  10.3 65.2 %all-to-all-start = ((bf16[128,2,8192]{2,1,0:T(2,128)(2,1)}), bf16[128,2,8192]{2,1,0:T(2,128)(2,1)}, u32[]{:S(2)}, u32[]{:S(2)}) async-start(bf16[128,2,8192]{2,1,0:T(2,128)(2,1)} %bitcast.215), calls=%async_computation | async-start | bytes 8388608 | tf_op jit(solution)/shard_map/all_to_all | solution.py:120
  136.1 10.8 %copy-start = (f32[2048,2048]{1,0:T(8,128)}, f32[2048,2048]{1,0:T(8,128)S(1)}, u32[]{:S(2)}) copy-start(f32[2048,2048]{1,0:T(8,128)S(1)} %fusion.121) | copy-start | bytes 50331652
  146.8 10.6 %copy-start.3 = (bf16[256,1024]{1,0:T(8,128)(2,1)S(1)}, bf16[256,1024]{1,0:T(8,128)(2,1)}, u32[]{:S(2)}) copy-start(bf16[256,1024]{1,0:T(8,128)(2,1)} %get-tuple-element.11) | copy-start | bytes 1572868
  147.6 19.3 %copy-start.2 = (bf16[256,1024]{1,0:T(8,128)(2,1)S(1)}, bf16[256,1024]{1,0:T(8,128)(2,1)}, u32[]{:S(2)}) copy-start(bf16[256,1024]{1,0:T(8,128)(2,1)} %get-tuple-element.10) | copy-start | bytes 1572868
  157.7 18.7 %copy-start.1 = (bf16[256,1024]{1,0:T(8,128)(2,1)S(1)}, bf16[256,1024]{1,0:T(8,128)(2,1)}, u32[]{:S(2)}) copy-start(bf16[256,1024]{1,0:T(8,128)(2,1)} %get-tuple-element.9) | copy-start | bytes 1572868
  286.1 19.9 %slice-start = ((s8[16777216]{0:T(1024)(128)(4,1)}), s8[4194304]{0:T(1024)(128)(4,1)S(1)}, s32[]{:S(2)}) async-start(s8[16777216]{0:T(1024)(128)(4,1)} %bitcast.211), calls=%async_computation.4 | async-start | bytes 8388608
  286.1 19.9 %slice-start.1 = ((s8[16777216]{0:T(1024)(128)(4,1)}), s8[4194304]{0:T(1024)(128)(4,1)S(1)}, s32[]{:S(2)}) async-start(s8[16777216]{0:T(1024)(128)(4,1)} %bitcast.211), calls=%async_computation.5 | async-start | bytes 8388608
  296.1 9.9 %slice-start.2 = ((s8[16777216]{0:T(1024)(128)(4,1)}), s8[4194304]{0:T(1024)(128)(4,1)S(1)}, s32[]{:S(2)}) async-start(s8[16777216]{0:T(1024)(128)(4,1)} %bitcast.211), calls=%async_computation.6 | async-start | bytes 8388608
  296.1 9.9 %slice-start.3 = ((s8[16777216]{0:T(1024)(128)(4,1)}), s8[4194304]{0:T(1024)(128)(4,1)S(1)}, s32[]{:S(2)}) async-start(s8[16777216]{0:T(1024)(128)(4,1)} %bitcast.211), calls=%async_computation.7 | async-start | bytes 8388608
  311.1 19.9 %slice-start.4 = ((s8[16777216]{0:T(1024)(128)(4,1)}), s8[4194304]{0:T(1024)(128)(4,1)S(1)}, s32[]{:S(2)}) async-start(s8[16777216]{0:T(1024)(128)(4,1)} %bitcast.213), calls=%async_computation.8 | async-start | bytes 8388608
  311.1 19.9 %slice-start.5 = ((s8[16777216]{0:T(1024)(128)(4,1)}), s8[4194304]{0:T(1024)(128)(4,1)S(1)}, s32[]{:S(2)}) async-start(s8[16777216]{0:T(1024)(128)(4,1)} %bitcast.213), calls=%async_computation.9 | async-start | bytes 8388608
  321.0 10.0 %slice-start.6 = ((s8[16777216]{0:T(1024)(128)(4,1)}), s8[4194304]{0:T(1024)(128)(4,1)S(1)}, s32[]{:S(2)}) async-start(s8[16777216]{0:T(1024)(128)(4,1)} %bitcast.213), calls=%async_computation.10 | async-start | bytes 8388608
  321.0 10.0 %slice-start.7 = ((s8[16777216]{0:T(1024)(128)(4,1)}), s8[4194304]{0:T(1024)(128)(4,1)S(1)}, s32[]{:S(2)}) async-start(s8[16777216]{0:T(1024)(128)(4,1)} %bitcast.213), calls=%async_computation.11 | async-start | bytes 8388608
  331.0 12.2 %copy-start.5 = (f32[256,1,8]{2,0,1:T(8,128)S(1)}, f32[256,1,8]{2,0,1:T(8,128)}, u32[]{:S(2)}) copy-start(f32[256,1,8]{2,0,1:T(8,128)} %stack_reshape.56) | copy-start | bytes 24580
  338.7 14.3 %all-to-all-start.3 = ((f32[128,1,128]{2,1,0:T(1,128)}), f32[128,1,128]{2,1,0:T(1,128)S(1)}, u32[]{:S(2)}, u32[]{:S(2)}) async-start(f32[128,1,128]{2,1,0:T(1,128)} %reshape.210), calls=%async_computation.3 | async-start | bytes 131072 | tf_op jit(solution)/shard_map/all_to_all | solution.py:132
  352.9 32.6 %all-to-all-start.1 = ((f32[128,1,128]{2,1,0:T(1,128)}), f32[128,1,128]{2,1,0:T(1,128)S(1)}, u32[]{:S(2)}, u32[]{:S(2)}) async-start(f32[128,1,128]{2,1,0:T(1,128)} %reshape.208), calls=%async_computation.1 | async-start | bytes 131072 | tf_op jit(solution)/shard_map/all_to_all | solution.py:139
  374.9 21.3 %copy-start.9 = (s32[8]{0:T(128)S(1)}, s32[8]{0:T(128)}, u32[]{:S(2)}) copy-start(s32[8]{0:T(128)} %param.17) | copy-start | bytes 100
  374.9 21.4 %copy-start.4 = (bf16[8,8192]{1,0:T(8,128)(2,1)S(1)}, bf16[8,8192]{1,0:T(8,128)(2,1)}, u32[]{:S(2)}) copy-start(bf16[8,8192]{1,0:T(8,128)(2,1)} %param.10) | copy-start | bytes 393220
  385.5 17.1 %copy-start.8 = (s32[8]{0:T(128)S(1)}, s32[8]{0:T(128)}, u32[]{:S(2)}) copy-start(s32[8]{0:T(128)} %copy-done.7) | copy-start | bytes 100
  385.5 109.5 %all-to-all-start.2 = ((f32[128,2,8192]{2,1,0:T(2,128)}), f32[128,2,8192]{2,1,0:T(2,128)}, u32[]{:S(2)}, u32[]{:S(2)}) async-start(f32[128,2,8192]{2,1,0:T(2,128)} %reshape_reshape.14), calls=%async_computation.2 | async-start | bytes 16777216 | tf_op jit(solution)/shard_map/all_to_all | solution.py:125
  396.2 14.7 %copy-start.6 = (pred[8]{0:T(512)(128)(4,1)S(1)}, pred[8]{0:T(512)(128)(4,1)}, u32[]{:S(2)}) copy-start(pred[8]{0:T(512)(128)(4,1)} %get-tuple-element.35) | copy-start | bytes 28
where the time goes:
time: 519 us; the launch traced here: 514 us
  matrix products  185 us (36%)
  waiting for transfers between devices  143 us (28%)
  local copies, waits for them, and re-layouts  105 us (20%)
  other arithmetic  46.3 us (9%)
  starting transfers between devices  32.2 us (6%)
    dot_general x8, matrix products, block_partials(): lax.dot_general(query_rows, keys_here[0, kv_index], (((1,), (1,)), ((), (...  105 us
    all_to_all x1, waiting for transfers between devices, local(): lax.all_to_all(block_out.reshape(owners * members, CAP, head_count * head...  83.7 us
    dot_general x8, matrix products, block_partials(): jnp.dot(weights.astype(jnp.bfloat16), values_here[0, kv_index], preferred...  69.2 us
    all_to_all x1, waiting for transfers between devices, local(): lax.all_to_all(copies, ('prefix', 'row'), split_axis=0, concat_axis=0, ti...  52 us
    slice x1, local copies, waits for them, and re-layouts, block_partials(): query_rows = grouped[:, kv_index].reshape(slot_count * groups, head_dim)  48.9 us
    reduce_sum x1, other arithmetic, block_partials(): totals.append(jnp.sum(weights, axis=1).reshape(slot_count, groups))  35.6 us
    all_to_all x1, starting transfers between devices, local(): lax.all_to_all(copies, ('prefix', 'row'), split_axis=0, concat_axis=0, ti...  12.6 us
    reshape x1, local copies, waits for them, and re-layouts, local(): back_out.reshape(owners, members, CAP, head_count, head_dim)  11.8 us
  transfers between devices with their start and end apart: 4, of which 3 were waited for; matrix products, arithmetic and copies ran while one was open for 9% of the time, Pallas kernels for 0%

commit v1 on v0

v1 whole, which is shorter than its diff:
```python
import functools
import math

import jax
import jax.numpy as jnp
from jax import lax
from jax.experimental import pallas as pl
from jax.experimental.pallas import tpu as pltpu
from jax.sharding import Mesh, PartitionSpec as P

AXES = ("z", "x", "y", "c")
CAP = 2
OWNERS = 16
HD = 128
GROUPS = 8
KV_HALF = 4
HEADS_HALF = 32
HALF = HEADS_HALF * HD
WIDE = HALF + HD
BLOCK = 2048
CHIP_SPAN = 2 * BLOCK
MASKED = -1e30
SCALE = math.log2(math.e) / math.sqrt(HD)
NT = (((1,), (1,)), ((), ()))
F32 = jnp.float32
BF16 = jnp.bfloat16


def lanes(shape):
    return lax.broadcasted_iota(jnp.int32, shape, len(shape) - 1)


def split_three(value, lane):
    high = value.astype(BF16).astype(F32)
    rest = value - high
    middle = rest.astype(BF16).astype(F32)
    low = rest - middle
    return jnp.where(lane < 32, high, jnp.where(lane < 64, middle, low)).astype(BF16)


def join_three(block):
    wide = block.astype(F32)
    return wide + pltpu.roll(wide, 96, 1) + pltpu.roll(wide, 64, 1)


def dispatch_kernel(ids, core_ref, q_ref, mine_ref, other_ref, pick_ref):
    core = core_ref[0]
    rows = q_ref.shape[0]
    row = lax.broadcasted_iota(jnp.int32, (OWNERS * CAP, rows), 0)
    column = lanes((OWNERS * CAP, rows))
    pick_row = lax.broadcasted_iota(jnp.int32, (rows, HD), 0)
    pick_lane = lanes((rows, HD))
    placing = jnp.zeros((OWNERS * CAP, rows), F32)
    pick = jnp.zeros((rows, HD), F32)
    for i in range(rows):
        slot = ids[i] * CAP
        for e in range(i):
            slot = slot + (ids[e] == ids[i]).astype(jnp.int32)
        placing = jnp.where((row == slot) & (column == i), 1.0, placing)
        pick = jnp.where((pick_lane == slot) & (pick_row == i), 1.0, pick)
    placing = placing.astype(BF16)
    pick_ref[...] = pick.astype(BF16)
    flags = jnp.ones((rows, HD), BF16)
    for target, half in ((mine_ref, core), (other_ref, 1 - core)):
        part = q_ref[:, pl.ds(pl.multiple_of(half * HALF, HALF), HALF)]
        target[:, :HALF] = jnp.dot(placing, part, preferred_element_type=F32).astype(BF16)
        target[:, HALF:] = jnp.dot(placing, flags, preferred_element_type=F32).astype(BF16)


def dispatch(queries, prefix_ids, core):
    rows = queries.shape[0]
    slots = OWNERS * CAP
    return pl.pallas_call(
        dispatch_kernel,
        in_specs=[
            pl.BlockSpec(memory_space=pltpu.SMEM),
            pl.BlockSpec(memory_space=pltpu.SMEM),
            pl.BlockSpec(memory_space=pltpu.VMEM),
        ],
        out_specs=[pl.BlockSpec(memory_space=pltpu.VMEM)] * 3,
        out_shape=[
            jax.ShapeDtypeStruct((slots, WIDE), BF16),
            jax.ShapeDtypeStruct((slots, WIDE), BF16),
            jax.ShapeDtypeStruct((rows, HD), BF16),
        ],
        name="dispatch",
    )(prefix_ids, core, queries)


def suffix_kernel(lengths, q_ref, k_ref, v_ref, o_ref, lse_ref):
    i = pl.program_id(0)
    length = lengths[i]
    span = k_ref.shape[2]
    kv_heads = k_ref.shape[1]
    heads = kv_heads * GROUPS
    scores = [
        lax.dot_general(
            q_ref[0, k * GROUPS : (k + 1) * GROUPS], k_ref[0, k], NT, preferred_element_type=F32
        )
        for k in range(kv_heads)
    ]
    scores = jnp.concatenate(scores, axis=0) * SCALE
    valid = lanes((heads, span)) < length
    scores = jnp.where(valid, scores, MASKED)
    peak = jnp.max(scores, axis=1, keepdims=True)
    weights = jnp.where(valid, jnp.exp2(scores - peak), 0.0)
    total = jnp.sum(weights, axis=1, keepdims=True)
    rounded = weights.astype(BF16)
    outs = [
        jnp.dot(rounded[k * GROUPS : (k + 1) * GROUPS], v_ref[0, k], preferred_element_type=F32)
        for k in range(kv_heads)
    ]
    out = jnp.concatenate(outs, axis=0) / total
    here = lax.broadcasted_iota(jnp.int32, lse_ref.shape, 0) == i
    for h in range(heads):
        place = slice(h * HD, (h + 1) * HD)
        o_ref[:, place] = jnp.where(here, out[h : h + 1], o_ref[:, place])
    lse = jnp.broadcast_to(peak + jnp.log2(total), (heads, HD))
    diagonal = lax.broadcasted_iota(jnp.int32, (heads, HD), 0) == lanes((heads, HD))
    row = jnp.sum(jnp.where(diagonal, lse, 0.0), axis=0, keepdims=True)
    lse_ref[...] = jnp.where(here, row, lse_ref[...])


def suffix(queries, keys, values, lengths):
    rows, kv_heads, span, hd = keys.shape
    heads = kv_heads * GROUPS
    return pl.pallas_call(
        suffix_kernel,
        grid_spec=pltpu.PrefetchScalarGridSpec(
            num_scalar_prefetch=1,
            grid=(rows,),
            in_specs=[
                pl.BlockSpec((1, heads, hd), lambda i, *_: (i, 0, 0)),
                pl.BlockSpec((1, kv_heads, span, hd), lambda i, *_: (i, 0, 0, 0)),
                pl.BlockSpec((1, kv_heads, span, hd), lambda i, *_: (i, 0, 0, 0)),
            ],
            out_specs=[
                pl.BlockSpec((rows, heads * hd), lambda i, *_: (0, 0)),
                pl.BlockSpec((rows, hd), lambda i, *_: (0, 0)),
            ],
        ),
        out_shape=[
            jax.ShapeDtypeStruct((rows, heads * hd), F32),
            jax.ShapeDtypeStruct((rows, hd), F32),
        ],
        compiler_params=pltpu.CompilerParams(vmem_limit_bytes=24 << 20),
        cost_estimate=pl.CostEstimate(
            flops=4 * rows * heads * span * hd,
            bytes_accessed=4 * rows * kv_heads * span * hd,
            transcendentals=rows * heads * span,
        ),
        name="suffix",
    )(lengths, queries.reshape(rows, heads, hd), keys, values)


def prefix_kernel(
    meta, x_ref, k_own, v_own, k_peer, v_peer, o_ref, keys, values, m_ref, lse_ref, sems
):
    length = meta[0]
    core = meta[1]
    count = x_ref.shape[0]
    rows = GROUPS * count
    sub = min(256, rows)
    own = pl.ds(pl.multiple_of(core * BLOCK, BLOCK), BLOCK)
    peer = pl.ds(pl.multiple_of((1 - core) * BLOCK, BLOCK), BLOCK)

    def copies(j):
        return (
            pltpu.make_async_copy(k_own.at[core * KV_HALF + j], keys.at[j, own], sems.at[j, 0]),
            pltpu.make_async_copy(k_peer.at[j], keys.at[j, peer], sems.at[j, 1]),
            pltpu.make_async_copy(v_own.at[core * KV_HALF + j], values.at[j, own], sems.at[j, 2]),
            pltpu.make_async_copy(v_peer.at[j], values.at[j, peer], sems.at[j, 3]),
        )

    for j in range(KV_HALF):
        for copy in copies(j):
            copy.start()

    def step(j, q, first, span, masked, accs):
        place = pl.ds(pl.multiple_of(first, span), span)
        key = keys[j, place, :]
        value = values[j, place, :]
        ones = jnp.ones((span, HD), BF16)
        if masked:
            inside = first + lax.broadcasted_iota(jnp.int32, (span, HD), 0) < length
            value = jnp.where(inside, value, jnp.zeros_like(value))
            ones = jnp.where(inside, ones, jnp.zeros_like(ones))
        value = jnp.concatenate([value, ones], axis=1)
        out = []
        for u in range(rows // sub):
            part = slice(u * sub, (u + 1) * sub)
            scores = lax.dot_general(q[part], key, NT, preferred_element_type=F32) * SCALE
            base = jnp.concatenate([m_ref[part, :]] * (span // HD), axis=1)
            weights = jnp.exp2(scores - base).astype(BF16)
            out.append(accs[u] + jnp.dot(weights, value, preferred_element_type=F32))
        return tuple(out)

    def head(j, _):
        for copy in copies(j):
            copy.wait()
        start = pl.multiple_of(j * GROUPS * HD, GROUPS * HD)
        q = jnp.concatenate(
            [x_ref[:, pl.ds(start + g * HD, HD)] for g in range(GROUPS)], axis=0
        )

        def peak_of(first):
            key = keys[j, pl.ds(pl.multiple_of(first, 256), 256), :]
            scores = lax.dot_general(q, key, NT, preferred_element_type=F32) * SCALE
            scores = jnp.where(first + lanes((rows, 256)) < length, scores, MASKED)
            return jnp.broadcast_to(jnp.max(scores, axis=1, keepdims=True), (rows, HD))

        m_ref[...] = peak_of(0)

        def attempt(state):
            turn = state[0]

            @pl.when(turn == 1)
            def _():
                def more(t, carry):
                    m_ref[...] = jnp.maximum(m_ref[...], peak_of(t * 256))
                    return carry

                lax.fori_loop(1, (length + 255) // 256, more, 0)

            accs = tuple(jnp.zeros((sub, 2 * HD), F32) for _ in range(rows // sub))
            whole = length // 2048
            accs = lax.fori_loop(
                0, whole, lambda t, a: step(j, q, t * 2048, 2048, False, a), accs
            )
            accs = lax.fori_loop(
                whole * 4,
                (length + 511) // 512,
                lambda t, a: step(j, q, t * 512, 512, True, a),
                accs,
            )
            acc = jnp.concatenate(accs, axis=0)
            total = acc[:, HD:]
            out = (acc[:, :HD] / total).astype(BF16)
            lse = m_ref[...] + jnp.log2(total)
            lane = lanes((count, HD)) % 32
            for g in range(GROUPS):
                part = slice(g * count, (g + 1) * count)
                o_ref[:, pl.ds(start + g * HD, HD)] = out[part]
                lse_ref[...] = jnp.where(lane == j * GROUPS + g, lse[part], lse_ref[...])
            wrong = jnp.sum(jnp.where(total < 1e30, 0.0, 1.0))
            return turn + 1, (wrong > 0.0).astype(jnp.int32)

        lax.while_loop(
            lambda state: (state[0] < 2) & (state[1] == 1), attempt, (jnp.int32(0), jnp.int32(1))
        )
        return 0

    @pl.when(length > 0)
    def _():
        lse_ref[...] = jnp.zeros_like(lse_ref)
        lax.fori_loop(0, KV_HALF, head, 0)

    @pl.when(length == 0)
    def _():
        for j in range(KV_HALF):
            for copy in copies(j):
                copy.wait()
        o_ref[:, :HALF] = jnp.zeros((count, HALF), BF16)
        lse_ref[...] = jnp.full_like(lse_ref, MASKED)

    o_ref[:, HALF:] = split_three(lse_ref[...], lanes((count, HD)))


def prefix_partial(x, meta, k_own, v_own, k_peer, v_peer):
    count = x.shape[0]
    any_space = pl.BlockSpec(memory_space=pl.ANY)
    return pl.pallas_call(
        prefix_kernel,
        in_specs=[
            pl.BlockSpec(memory_space=pltpu.SMEM),
            pl.BlockSpec(memory_space=pltpu.VMEM),
            any_space,
            any_space,
            any_space,
            any_space,
        ],
        out_specs=pl.BlockSpec(memory_space=pltpu.VMEM),
        out_shape=jax.ShapeDtypeStruct((count, WIDE), BF16),
        scratch_shapes=[
            pltpu.VMEM((KV_HALF, CHIP_SPAN, HD), BF16),
            pltpu.VMEM((KV_HALF, CHIP_SPAN, HD), BF16),
            pltpu.VMEM((GROUPS * count, HD), F32),
            pltpu.VMEM((count, HD), F32),
            pltpu.SemaphoreType.DMA((KV_HALF, 4)),
        ],
        compiler_params=pltpu.CompilerParams(vmem_limit_bytes=48 << 20),
        cost_estimate=pl.CostEstimate(
            flops=4 * 4 * count * HEADS_HALF * CHIP_SPAN * HD,
            bytes_accessed=16 * BLOCK * KV_HALF * HD,
            transcendentals=count * HEADS_HALF * CHIP_SPAN,
        ),
        name="prefix_partial",
    )(meta, x, k_own, v_own, k_peer, v_peer)


def merge_kernel(*refs):
    parts, out_ref = refs[:-1], refs[-1]
    sums = [join_three(part[:, HALF:]) for part in parts]
    top = functools.reduce(jnp.maximum, sums)
    shares = [jnp.exp2(s - top) for s in sums]
    whole = functools.reduce(jnp.add, shares)
    shares = [s / whole for s in shares]
    for h in range(HEADS_HALF):
        block = slice(h * HD, (h + 1) * HD)
        out = None
        for part, share in zip(parts, shares):
            term = part[:, block].astype(F32) * share[:, h : h + 1]
            out = term if out is None else out + term
        out_ref[:, block] = out.astype(BF16)
    lane = lanes(top.shape)
    lse = jnp.where(lane < 32, top + jnp.log2(whole), 0.0)
    lse = lse + pltpu.roll(lse, 32, 1) + pltpu.roll(lse, 64, 1)
    out_ref[:, HALF:] = split_three(lse, lane)


def merge(*parts):
    return pl.pallas_call(
        merge_kernel,
        out_shape=jax.ShapeDtypeStruct(parts[0].shape, BF16),
        name="merge",
    )(*parts)


def finish_kernel(core_ref, mine_ref, got_ref, pick_ref, o_ref, lse_ref, out_ref):
    core = core_ref[0]
    slots = mine_ref.shape[0]
    pick = pick_ref[:, :slots]
    mine = jnp.dot(pick, mine_ref[...], preferred_element_type=F32)
    got = jnp.dot(pick, got_ref[...], preferred_element_type=F32)
    lower = core == 0
    for half in range(2):
        own = lower if half == 0 else jnp.logical_not(lower)
        part = jnp.where(own, mine, got)
        prefix_lse = join_three(part[:, HALF:])
        suffix_lse = lse_ref[...]
        if half:
            suffix_lse = pltpu.roll(suffix_lse, 96, 1)
        top = jnp.maximum(prefix_lse, suffix_lse)
        prefix_share = jnp.exp2(prefix_lse - top)
        suffix_share = jnp.exp2(suffix_lse - top)
        whole = prefix_share + suffix_share
        prefix_share = prefix_share / whole
        suffix_share = suffix_share / whole
        for h in range(HEADS_HALF):
            block = slice(h * HD, (h + 1) * HD)
            place = slice(half * HALF + h * HD, half * HALF + (h + 1) * HD)
            out_ref[:, place] = (
                part[:, block] * prefix_share[:, h : h + 1]
                + o_ref[:, place] * suffix_share[:, h : h + 1]
            ).astype(BF16)


def finish(core, mine, got, pick, suffix_out, suffix_lse):
    space = pl.BlockSpec(memory_space=pltpu.VMEM)
    return pl.pallas_call(
        finish_kernel,
        in_specs=[pl.BlockSpec(memory_space=pltpu.SMEM)] + [space] * 5,
        out_specs=space,
        out_shape=jax.ShapeDtypeStruct(suffix_out.shape, BF16),
        name="finish",
    )(core, mine, got, pick, suffix_out, suffix_lse)


def ring(shift):
    return [(i, (i + shift) % 4) for i in range(4)]


SWAP = [(0, 1), (1, 0)]


def local(
    queries,
    prefix_ids,
    prefix_lengths,
    prefix_keys,
    prefix_values,
    suffix_keys,
    suffix_values,
    suffix_lengths,
):
    core = lax.axis_index("c")
    chip = lax.axis_index("y")
    core_array = core.reshape(1).astype(jnp.int32)
    keys = prefix_keys[0]
    values = prefix_values[0]
    k_peer = lax.ppermute(
        lax.dynamic_slice_in_dim(keys, (1 - core) * KV_HALF, KV_HALF, 0), "c", SWAP
    )
    v_peer = lax.ppermute(
        lax.dynamic_slice_in_dim(values, (1 - core) * KV_HALF, KV_HALF, 0), "c", SWAP
    )
    mine, other, pick = dispatch(queries, prefix_ids, core_array)
    got = lax.ppermute(other, "c", SWAP)
    leaving = jnp.concatenate(
        [mine.reshape(OWNERS, CAP, WIDE), got.reshape(OWNERS, CAP, WIDE)], axis=1
    )
    arrived = lax.all_to_all(leaving, ("z", "x"), split_axis=0, concat_axis=0, tiled=True)
    arrived = arrived.reshape(OWNERS * 2 * CAP, WIDE)
    suffix_out, suffix_lse = suffix(queries, suffix_keys, suffix_values, suffix_lengths)

    count = jnp.clip(prefix_lengths[0] - chip * CHIP_SPAN, 0, CHIP_SPAN)
    meta = jnp.stack([count, core]).astype(jnp.int32)
    work = functools.partial(
        prefix_partial, meta=meta, k_own=keys, v_own=values, k_peer=k_peer, v_peer=v_peer
    )
    from_left = lax.ppermute(arrived, "y", ring(1))
    from_right = lax.ppermute(arrived, "y", ring(3))
    from_far = lax.ppermute(arrived, "y", ring(2))
    size = arrived.shape[0]
    for_left = work(from_left)
    back_left = lax.ppermute(for_left, "y", ring(3))
    for_right = work(from_right)
    back_right = lax.ppermute(for_right, "y", ring(1))
    for_far = work(from_far)
    back_far = lax.ppermute(for_far, "y", ring(2))
    for_self = work(arrived)
    merged = merge(for_self, back_left, back_right, back_far)
    returned = lax.all_to_all(
        merged.reshape(OWNERS, 2 * CAP, WIDE), ("z", "x"), split_axis=0, concat_axis=0, tiled=True
    )
    mine_back = returned[:, :CAP].reshape(OWNERS * CAP, WIDE)
    got_back = lax.ppermute(returned[:, CAP:].reshape(OWNERS * CAP, WIDE), "c", SWAP)
    return finish(core_array, mine_back, got_back, pick, suffix_out, suffix_lse)


def solution(mesh):
    fine = Mesh(mesh.devices.reshape(4, 4, 4, 2), AXES)
    rows = P(AXES)
    placed = (
        P(AXES, None),
        rows,
        P(("z", "x")),
        P(("z", "x"), None, ("y", "c"), None),
        P(("z", "x"), None, ("y", "c"), None),
        P(AXES, None, None, None),
        P(AXES, None, None, None),
        rows,
    )
    return jax.shard_map(
        local, mesh=fine, in_specs=placed, out_specs=P(AXES, None), check_vma=False
    )
```

time: 519 us -> 167 us (0.32)
  matrix products: 185 us -> 0 us
  waiting for transfers between devices: 143 us -> 10.6 us
  local copies, waits for them, and re-layouts: 105 us -> 19 us
  Pallas kernels: 0 us -> 84.4 us
  other arithmetic: 46.3 us -> 0.64 us
  blocking collectives: 0 us -> 40.1 us
  starting transfers between devices: 32.2 us -> 11.7 us
    dot_general x19 -> x0, matrix products: 185 us -> none  [the longest x8 105 us: block_partials(): lax.dot_general(query_rows, keys_here[0, kv_index], (((1,), (1,)), ((), (...]
    all_to_all x4 -> x0, waiting for transfers between devices: 143 us -> none  [the longest x1 83.7 us: local(): lax.all_to_all(block_out.reshape(owners * members, CAP, head_count * head...]
    pallas_call x0 -> x8, Pallas kernels: none -> 84.4 us  [the longest x4 70.9 us: prefix_partial(): pl.pallas_call(prefix_kernel, in_specs=[pl.BlockSpec(memory_space=pltpu.S...]
    slice x1, local copies, waits for them, and re-layouts: 48.9 us -> 0.38 us  [local(): returned[:, CAP:].reshape(OWNERS * CAP, WIDE)]
    reduce_sum x5 -> x0, other arithmetic: 42.3 us -> none  [the longest x1 35.6 us: block_partials(): totals.append(jnp.sum(weights, axis=1).reshape(slot_count, groups))]
    all_to_all x0 -> x2, blocking collectives: none -> 40.1 us  [the longest x1 21.5 us: local(): lax.all_to_all(merged.reshape(OWNERS, 2 * CAP, WIDE), ('z', 'x'), split_a...]
    another operation x33 -> x0, local copies, waits for them, and re-layouts: 32.3 us -> none  [the longest x1 10.6 us: local(): block_out.reshape(owners * members, CAP, head_count * head_dim)]
    all_to_all x4 -> x0, starting transfers between devices: 32.2 us -> none  [the longest x1 12.6 us: local(): lax.all_to_all(copies, ('prefix', 'row'), split_axis=0, concat_axis=0, ti...]
  transfers between devices with their start and end apart: 4 -> 10, of which waited for: 3 -> 2; matrix products, arithmetic and copies ran while one was open for 9% -> 3% of each run, Pallas kernels for 0% -> 47%
where the time goes in v1:
time: 167 us
  Pallas kernels  84.4 us (51%)
  blocking collectives  40.1 us (24%)
  local copies, waits for them, and re-layouts  19 us (11%)
  starting transfers between devices  11.7 us (7%)
  waiting for transfers between devices  10.6 us (6%)
    pallas_call x4, Pallas kernels, prefix_partial(): pl.pallas_call(prefix_kernel, in_specs=[pl.BlockSpec(memory_space=pltpu.S...  70.9 us
    all_to_all x1, blocking collectives, local(): lax.all_to_all(merged.reshape(OWNERS, 2 * CAP, WIDE), ('z', 'x'), split_a...  21.5 us
    all_to_all x1, blocking collectives, local(): lax.all_to_all(leaving, ('z', 'x'), split_axis=0, concat_axis=0, tiled=True)  18.6 us
    unnamed x23, local copies, waits for them, and re-layouts  10.6 us
    ppermute x1, waiting for transfers between devices, local(): from_left = lax.ppermute(arrived, 'y', ring(1))  8.19 us
    pallas_call x1, Pallas kernels, suffix(): pl.pallas_call(suffix_kernel, grid_spec=pltpu.PrefetchScalarGridSpec(num_...  5.47 us
    ppermute x1, starting transfers between devices, local(): lax.ppermute(returned[:, CAP:].reshape(OWNERS * CAP, WIDE), 'c', SWAP)  5.07 us
    pallas_call x1, Pallas kernels, merge(): pl.pallas_call(merge_kernel, out_shape=jax.ShapeDtypeStruct(parts[0].shap...  3.68 us
  transfers between devices with their start and end apart: 10, of which 2 were waited for; matrix products, arithmetic and copies ran while one was open for 3% of the time, Pallas kernels for 47%

profile of v1, /device:TPU:1, one launch (start us, length us, event | category | flops | bytes accessed | tf_op | source)
XLA Modules:
  0.0 167.2 jit_solution(10681795213495570861)
XLA Ops:
  0.0 0.0 copy-start.6
  0.0 3.2 %dynamic-slice_bitcast_fusion.1 = bf16[4,2048,128]{2,1,0:T(8,128)(2,1)} fusion(bf16[1,8,2048,128]{3,2,1,0:T(8,128)(2,1)} %param.11, s32[]{:T(128)S(6)} %select_n.4), kind=kLoop, calls=%fused_computation.1 | loop fusion | bytes 4194308 | tf_op jit(solution)/shard_map/dynamic_slice | solution.py:392
  3.2 1.4 collective-permute-start.1
  4.6 0.0 copy-done.6
  4.6 1.5 dynamic-slice_bitcast_fusion
  6.1 0.0 collective-permute-start.2
  6.1 2.0 %dispatch.1 = (bf16[32,4224]{1,0:T(8,128)(2,1)}, bf16[32,4224]{1,0:T(8,128)(2,1)}, bf16[8,128]{1,0:T(8,128)(2,1)}) custom-call(s32[8]{0:T(128)} %ids.1, s32[1]{0:T(128)} %bitcast.core_ref, bf16[8,8192]{1,0:T(8,128)(2,1)} %q_ref.1), custom_call_target="tpu_custom_call" | custom-call | tf_op jit(solution)/shard_map/dispatch/pallas_call | solution.py:73
  8.0 0.5 collective-permute-start
  8.5 1.1 reshape.27
  9.6 2.4 %collective-permute-done = bf16[32,4224]{1,0:T(8,128)(2,1)S(1)} collective-permute-done((bf16[32,4224]{1,0:T(8,128)(2,1)}, bf16[32,4224]{1,0:T(8,128)(2,1)S(1)}, u32[]{:S(2)}, u32[]{:S(2)}) %collective-permute-start) | collective-permute-done | bytes 270368 | tf_op jit(solution)/shard_map/ppermute | solution.py:398
  12.0 0.1 reshape.28
  12.1 0.6 pad_maximum_fusion
  12.7 18.6 %all_to_all.10 = bf16[16,4,4224]{2,1,0:T(4,128)(2,1)S(1)} all-to-all(bf16[16,4,4224]{2,1,0:T(4,128)(2,1)S(1)} %pad_maximum_fusion), channel_id=1, replica_groups=mesh['z'=4,'x'=4,'y'=4,'c'=2] {'z','x'}, dimensions={0} | all-to-all | bytes 1081344 | tf_op jit(solution)/shard_map/all_to_all | solution.py:402
  31.2 0.1 reshape.29.x_ref
  31.3 1.4 collective-permute-start.3
  33.4 0.1 pad_add_fusion.meta
  33.4 1.5 collective-permute-start.5
  34.9 1.6 collective-permute-start.7
  36.5 8.2 %collective-permute-done.3.x_ref = bf16[64,4224]{1,0:T(8,128)(2,1)S(1)} collective-permute-done((bf16[64,4224]{1,0:T(8,128)(2,1)S(1)}, bf16[64,4224]{1,0:T(8,128)(2,1)S(1)}, u32[]{:S(2)}, u32[]{:S(2)}) %collective-permute-start.3) | collective-permute-done | bytes 540704 | tf_op jit(solution)/shard_map/ppermute | solution.py:411
  44.7 0.0 collective-permute-done.1.k_peer
  44.7 0.0 collective-permute-done.2.v_peer
  44.7 17.7 %prefix_partial.5 = bf16[64,4224]{1,0:T(8,128)(2,1)S(1)} custom-call(s32[2]{0:T(128)S(1)} %pad_add_fusion.meta, bf16[64,4224]{1,0:T(8,128)(2,1)S(1)} %collective-permute-done.3.x_ref, bf16[8,2048,128]{2,1,0:T(8,128)(2,1)} %bitcast.15, bf16[8,2048,128]{2,1,0:T(8,128)(2,1)} %bitcast.19, bf16[4,2048,128]{2,1,0:T(8,128)(2,1)S(1)} %collective-permute-done.1.k_peer, ...), custom_call_target="tpu_custom_call" | custom-call | flops 17179869184 | bytes 16777216 | tf_op jit(solution)/shard_map/prefix_partial/pallas_call | solution.py:272
  62.5 0.1 collective-permute-start.4
  62.6 0.0 collective-permute-done.5.x_ref
  62.6 17.7 %prefix_partial.6 = bf16[64,4224]{1,0:T(8,128)(2,1)S(1)} custom-call(s32[2]{0:T(128)S(1)} %pad_add_fusion.meta, bf16[64,4224]{1,0:T(8,128)(2,1)S(1)} %collective-permute-done.5.x_ref, bf16[8,2048,128]{2,1,0:T(8,128)(2,1)} %bitcast.16, bf16[8,2048,128]{2,1,0:T(8,128)(2,1)} %bitcast.20, bf16[4,2048,128]{2,1,0:T(8,128)(2,1)S(1)} %collective-permute-done.1.k_peer, ...), custom_call_target="tpu_custom_call" | custom-call | flops 17179869184 | bytes 16777216 | tf_op jit(solution)/shard_map/prefix_partial/pallas_call | solution.py:272
  80.3 0.1 collective-permute-start.6
  80.4 0.0 collective-permute-done.7.x_ref
  80.4 17.7 %prefix_partial.7 = bf16[64,4224]{1,0:T(8,128)(2,1)S(1)} custom-call(s32[2]{0:T(128)S(1)} %pad_add_fusion.meta, bf16[64,4224]{1,0:T(8,128)(2,1)S(1)} %collective-permute-done.7.x_ref, bf16[8,2048,128]{2,1,0:T(8,128)(2,1)} %bitcast.17, bf16[8,2048,128]{2,1,0:T(8,128)(2,1)} %bitcast.21, bf16[4,2048,128]{2,1,0:T(8,128)(2,1)S(1)} %collective-permute-done.1.k_peer, ...), custom_call_target="tpu_custom_call" | custom-call | flops 17179869184 | bytes 16777216 | tf_op jit(solution)/shard_map/prefix_partial/pallas_call | solution.py:272
  98.1 0.1 collective-permute-start.8
  98.2 17.7 %prefix_partial.4.refs_0_ = bf16[64,4224]{1,0:T(8,128)(2,1)S(1)} custom-call(s32[2]{0:T(128)S(1)} %pad_add_fusion.meta, bf16[64,4224]{1,0:T(8,128)(2,1)S(1)} %reshape.29.x_ref, bf16[8,2048,128]{2,1,0:T(8,128)(2,1)} %bitcast.18, bf16[8,2048,128]{2,1,0:T(8,128)(2,1)} %bitcast.22, bf16[4,2048,128]{2,1,0:T(8,128)(2,1)S(1)} %collective-permute-done.1.k_peer, ...), custom_call_target="tpu_custom_call" | custom-call | flops 17179869184 | bytes 16777216 | tf_op jit(solution)/shard_map/prefix_partial/pallas_call | solution.py:272
  116.0 0.0 copy-start.2
  116.0 0.8 copy-done.2
  116.8 0.0 collective-permute-done.4.refs_1_
  116.8 0.0 copy-start.7
  116.8 0.0 collective-permute-done.6.refs_2_
  116.8 0.0 copy-start.8
  116.8 0.9 copy-done.8
  117.7 0.0 collective-permute-done.8.refs_3_
  117.7 0.1 copy-done.7
  117.8 3.7 %merge.1 = bf16[64,4224]{1,0:T(8,128)(2,1)} custom-call(bf16[64,4224]{1,0:T(8,128)(2,1)} %copy-done.2, bf16[64,4224]{1,0:T(8,128)(2,1)} %copy-done.7, bf16[64,4224]{1,0:T(8,128)(2,1)} %copy-done.8, bf16[64,4224]{1,0:T(8,128)(2,1)} %collective-permute-done.8.refs_3_), custom_call_target="tpu_custom_call" | custom-call | tf_op jit(solution)/shard_map/merge/pallas_call | solution.py:322
  121.5 0.0 copy-start.9
  121.5 0.0 copy-start.5
  121.5 1.2 reshape.30
  122.7 21.5 %all_to_all.11 = bf16[16,4,4224]{2,1,0:T(4,128)(2,1)S(1)} all-to-all(bf16[16,4,4224]{2,1,0:T(4,128)(2,1)S(1)} %reshape.30), channel_id=1, replica_groups=mesh['z'=4,'x'=4,'y'=4,'c'=2] {'z','x'}, dimensions={0} | all-to-all | bytes 1081344 | tf_op jit(solution)/shard_map/all_to_all | solution.py:423
  144.2 0.4 fusion
  144.6 0.1 reshape.32
  144.7 5.1 %collective-permute-start.9 = (bf16[32,4224]{1,0:T(8,128)(2,1)S(1)}, bf16[32,4224]{1,0:T(8,128)(2,1)S(1)}, u32[]{:S(2)}, u32[]{:S(2)}) collective-permute-start(bf16[32,4224]{1,0:T(8,128)(2,1)S(1)} %reshape.32), channel_id=1, source_target_pairs={{0,1},{1,0},{2,3},{3,2},{4,5},{5,4},{6,7},{7,6},{8,9},{9,8},{10,11... | collective-permute-start | bytes 811016 | tf_op jit(solution)/shard_map/ppermute | solution.py:427
  149.8 0.0 copy-done.9
  149.8 0.0 copy-done.5
  149.8 0.0 copy-start
  149.8 3.4 %copy-done = bf16[8,8,512,128]{3,2,1,0:T(8,128)(2,1)S(1)} copy-done((bf16[8,8,512,128]{3,2,1,0:T(8,128)(2,1)S(1)}, bf16[8,8,512,128]{3,2,1,0:T(8,128)(2,1)}, u32[]{:S(2)}) %copy-start) | copy-done | bytes 8388632
  153.2 0.0 copy-start.1
  153.2 3.4 %copy-done.1 = bf16[8,8,512,128]{3,2,1,0:T(8,128)(2,1)S(1)} copy-done((bf16[8,8,512,128]{3,2,1,0:T(8,128)(2,1)S(1)}, bf16[8,8,512,128]{3,2,1,0:T(8,128)(2,1)}, u32[]{:S(2)}) %copy-start.1) | copy-done | bytes 8388632
  156.6 5.5 %suffix.1 = (f32[8,8192]{1,0:T(8,128)S(1)}, f32[8,128]{1,0:T(8,128)S(1)}) custom-call(s32[8]{0:T(128)S(1)} %copy-done.5, bf16[8,64,128]{2,1,0:T(8,128)(2,1)S(1)} %bitcast.14, bf16[8,8,512,128]{3,2,1,0:T(8,128)(2,1)S(1)} %copy-done, bf16[8,8,512,128]{3,2,1,0:T(8,128)(2,1)S(1)} %copy-done.1), custom_call_target="tpu_custom_call" | custom-call | flops 134217728 | bytes 16777216 | tf_op jit(solution)/shard_map/suffix/pallas_call | solution.py:127
  162.1 0.0 copy-start.3
  162.1 0.7 copy-done.3
  162.8 0.0 copy-start.4
  162.8 0.6 copy-done.4
  163.4 0.8 reshape.31.mine_ref
  164.2 0.0 collective-permute-done.9.got_ref
  164.2 0.0 copy-start.10
  164.2 0.7 copy-done.10
  164.9 2.4 %finish.1 = bf16[8,8192]{1,0:T(8,128)(2,1)} custom-call(s32[1]{0:T(128)} %bitcast.core_ref, bf16[32,4224]{1,0:T(8,128)(2,1)} %reshape.31.mine_ref, bf16[32,4224]{1,0:T(8,128)(2,1)} %copy-done.10, bf16[8,128]{1,0:T(8,128)(2,1)} %get-tuple-element.12.pick_ref, f32[8,8192]{1,0:T(8,128)} %copy-done.3, f32[8,128]{1,0:T(8,128)} %copy-done.4), custom_call_target="tpu_custom_call" | custom-call | tf_op jit(solution)/shard_map/finish/pallas_call | solution.py:360
  (1 shorter events, 0.0 us)
Async XLA Ops:
  0.0 4.6 %copy-start.6 = (bf16[1,8,2048,128]{3,2,1,0:T(8,128)(2,1)S(1)}, bf16[1,8,2048,128]{3,2,1,0:T(8,128)(2,1)}, u32[]{:S(2)}) copy-start(bf16[1,8,2048,128]{3,2,1,0:T(8,128)(2,1)} %param.12) | copy-start | bytes 12582916
  3.2 41.5 %collective-permute-start.1 = (bf16[4,2048,128]{2,1,0:T(8,128)(2,1)}, bf16[4,2048,128]{2,1,0:T(8,128)(2,1)S(1)}, u32[]{:S(2)}, u32[]{:S(2)}) collective-permute-start(bf16[4,2048,128]{2,1,0:T(8,128)(2,1)} %dynamic-slice_bitcast_fusion.1), channel_id=1, source_target_pairs={{0,1},{1,0},{2,3},{3,2},{4,5},{5,4},{6,7},{7,6},{8,9},{9,8},{10,11... | collective-permute-start | bytes 6291464 | tf_op jit(solution)/shard_map/ppermute | solution.py:391
  6.1 38.7 %collective-permute-start.2 = (bf16[4,2048,128]{2,1,0:T(8,128)(2,1)}, bf16[4,2048,128]{2,1,0:T(8,128)(2,1)}, u32[]{:S(2)}, u32[]{:S(2)}) collective-permute-start(bf16[4,2048,128]{2,1,0:T(8,128)(2,1)} %dynamic-slice_bitcast_fusion), channel_id=1, source_target_pairs={{0,1},{1,0},{2,3},{3,2},{4,5},{5,4},{6,7},{7,6},{8,9},{9,8},{10,11... | collective-permute-start | bytes 6291464 | tf_op jit(solution)/shard_map/ppermute | solution.py:394
  8.0 3.9 %collective-permute-start = (bf16[32,4224]{1,0:T(8,128)(2,1)}, bf16[32,4224]{1,0:T(8,128)(2,1)S(1)}, u32[]{:S(2)}, u32[]{:S(2)}) collective-permute-start(bf16[32,4224]{1,0:T(8,128)(2,1)} %get-tuple-element.11), channel_id=1, source_target_pairs={{0,1},{1,0},{2,3},{3,2},{4,5},{5,4},{6,7},{7,6},{8,9},{9,8},{10,11... | collective-permute-start | bytes 811016 | tf_op jit(solution)/shard_map/ppermute | solution.py:398
  31.3 13.4 %collective-permute-start.3 = (bf16[64,4224]{1,0:T(8,128)(2,1)S(1)}, bf16[64,4224]{1,0:T(8,128)(2,1)S(1)}, u32[]{:S(2)}, u32[]{:S(2)}) collective-permute-start(bf16[64,4224]{1,0:T(8,128)(2,1)S(1)} %reshape.29.x_ref), channel_id=1, source_target_pairs={{0,2},{2,4},{4,6},{6,0},{1,3},{3,5},{5,7},{7,1},{8,10},{10,12},{12... | collective-permute-start | bytes 1622024 | tf_op jit(solution)/shard_map/ppermute | solution.py:411
  33.4 29.1 %collective-permute-start.5 = (bf16[64,4224]{1,0:T(8,128)(2,1)S(1)}, bf16[64,4224]{1,0:T(8,128)(2,1)S(1)}, u32[]{:S(2)}, u32[]{:S(2)}) collective-permute-start(bf16[64,4224]{1,0:T(8,128)(2,1)S(1)} %reshape.29.x_ref), channel_id=1, source_target_pairs={{0,6},{2,0},{4,2},{6,4},{1,7},{3,1},{5,3},{7,5},{8,14},{10,8},{12,... | collective-permute-start | bytes 1622024 | tf_op jit(solution)/shard_map/ppermute | solution.py:412
  34.9 45.5 %collective-permute-start.7 = (bf16[64,4224]{1,0:T(8,128)(2,1)S(1)}, bf16[64,4224]{1,0:T(8,128)(2,1)S(1)}, u32[]{:S(2)}, u32[]{:S(2)}) collective-permute-start(bf16[64,4224]{1,0:T(8,128)(2,1)S(1)} %reshape.29.x_ref), channel_id=1, source_target_pairs={{0,4},{2,6},{4,0},{6,2},{1,5},{3,7},{5,1},{7,3},{8,12},{10,14},{12... | collective-permute-start | bytes 1622024 | tf_op jit(solution)/shard_map/ppermute | solution.py:413
  62.5 54.3 %collective-permute-start.4 = (bf16[64,4224]{1,0:T(8,128)(2,1)S(1)}, bf16[64,4224]{1,0:T(8,128)(2,1)S(1)}, u32[]{:S(2)}, u32[]{:S(2)}) collective-permute-start(bf16[64,4224]{1,0:T(8,128)(2,1)S(1)} %prefix_partial.5), channel_id=1, source_target_pairs={{0,6},{2,0},{4,2},{6,4},{1,7},{3,1},{5,3},{7,5},{8,14},{10,8},{12,... | collective-permute-start | bytes 1622024 | tf_op jit(solution)/shard_map/ppermute | solution.py:416
  80.3 36.5 %collective-permute-start.6 = (bf16[64,4224]{1,0:T(8,128)(2,1)S(1)}, bf16[64,4224]{1,0:T(8,128)(2,1)S(1)}, u32[]{:S(2)}, u32[]{:S(2)}) collective-permute-start(bf16[64,4224]{1,0:T(8,128)(2,1)S(1)} %prefix_partial.6), channel_id=1, source_target_pairs={{0,2},{2,4},{4,6},{6,0},{1,3},{3,5},{5,7},{7,1},{8,10},{10,12},{12... | collective-permute-start | bytes 1622024 | tf_op jit(solution)/shard_map/ppermute | solution.py:418
  98.1 19.5 %collective-permute-start.8 = (bf16[64,4224]{1,0:T(8,128)(2,1)S(1)}, bf16[64,4224]{1,0:T(8,128)(2,1)}, u32[]{:S(2)}, u32[]{:S(2)}) collective-permute-start(bf16[64,4224]{1,0:T(8,128)(2,1)S(1)} %prefix_partial.7), channel_id=1, source_target_pairs={{0,4},{2,6},{4,0},{6,2},{1,5},{3,7},{5,1},{7,3},{8,12},{10,14},{12... | collective-permute-start | bytes 1622024 | tf_op jit(solution)/shard_map/ppermute | solution.py:420
  116.0 0.8 copy-start.2
  116.8 1.0 copy-start.7
  116.8 0.9 copy-start.8
  121.5 28.3 %copy-start.9 = (bf16[8,8192]{1,0:T(8,128)(2,1)S(1)}, bf16[8,8192]{1,0:T(8,128)(2,1)}, u32[]{:S(2)}) copy-start(bf16[8,8192]{1,0:T(8,128)(2,1)} %q_ref.1) | copy-start | bytes 393220
  121.5 28.3 %copy-start.5 = (s32[8]{0:T(128)S(1)}, s32[8]{0:T(128)}, u32[]{:S(2)}) copy-start(s32[8]{0:T(128)} %lengths.1) | copy-start | bytes 100
  144.7 19.4 %collective-permute-start.9 = (bf16[32,4224]{1,0:T(8,128)(2,1)S(1)}, bf16[32,4224]{1,0:T(8,128)(2,1)S(1)}, u32[]{:S(2)}, u32[]{:S(2)}) collective-permute-start(bf16[32,4224]{1,0:T(8,128)(2,1)S(1)} %reshape.32), channel_id=1, source_target_pairs={{0,1},{1,0},{2,3},{3,2},{4,5},{5,4},{6,7},{7,6},{8,9},{9,8},{10,11... | collective-permute-start | bytes 811016 | tf_op jit(solution)/shard_map/ppermute | solution.py:427
  149.8 3.4 %copy-start = (bf16[8,8,512,128]{3,2,1,0:T(8,128)(2,1)S(1)}, bf16[8,8,512,128]{3,2,1,0:T(8,128)(2,1)}, u32[]{:S(2)}) copy-start(bf16[8,8,512,128]{3,2,1,0:T(8,128)(2,1)} %k_ref.1) | copy-start | bytes 25165828
  153.2 3.4 %copy-start.1 = (bf16[8,8,512,128]{3,2,1,0:T(8,128)(2,1)S(1)}, bf16[8,8,512,128]{3,2,1,0:T(8,128)(2,1)}, u32[]{:S(2)}) copy-start(bf16[8,8,512,128]{3,2,1,0:T(8,128)(2,1)} %v_ref.1) | copy-start | bytes 25165828
  162.1 0.7 copy-start.3
  162.8 0.6 copy-start.4
  164.2 0.7 copy-start.10
